TPU v7x, 512 devices: a whole 4x8x8 slice. The times are simulated.
512 devices in a mesh: tm: 16 (over y, core), space: 32 (over x, z).
Axes of the slice: x: 4, y: 8, z: 8, core: 2. Of those that a mesh axis runs over, the one named last changes fastest.
Arguments:
- coupling: bfloat16 [16, 2048, 2048], P('tm', 'space'), may hold values from -0.125 to 0.125
- arrow_link: float32 [16, 2048, 64], P('tm'), may hold values from -0.75 to 0.75
- local_cov: float32 [16, 2048, 2048], P('tm', 'space'), as said below
- boundary_cov: float32 [16, 2048, 2048], P('tm', 'space'), as said below
- boundary_arrow: float32 [16, 2048, 64], P('tm', 'space'), may hold values from -6 to 6
- fixed_cov: float32 [64, 64], replicated, as said below
Outputs:
- diag_blocks: float32 [16, 2048, 2048], P('tm', 'space')
- cross_blocks: float32 [16, 2048, 2048], P('tm', 'space')
- arrow_covs: float32 [16, 2048, 64], P('tm', 'space')
Inputs may be any that keep to these rules, and one draw needn't show every extreme that they name: `local_cov`: each block is symmetric. `boundary_cov`: each block is symmetric. `fixed_cov`: symmetric.
All inputs are finite; a program needn't handle non-finite values.
Results may differ from a plain program's by a relative error of at most 0.0003.
Values may be sent and summed in bfloat16 or wider, within the bound.
No kernel may reach another device: no remote copies, remote signals or barrier semaphores. Data moves between devices by JAX's collectives and lax.ppermute only.
A program may use at most 64 MiB of HBM per device.

v0:
```python
import jax
import jax.numpy as jnp
from jax import lax
from jax.sharding import PartitionSpec as P


def passed_along(block, axis, distance):
    devices = range(lax.axis_size(axis))
    route = [(i - distance, i) for i in devices if i - distance in devices]
    return lax.ppermute(block, axis, route)


def shards(coupling, arrow_link, local_cov, boundary_cov, boundary_arrow, fixed_cov):
    highest = lax.Precision.HIGHEST
    next_block, next_arrow = passed_along((boundary_cov, boundary_arrow), "tm", -1)
    panels = lax.all_gather(coupling, "space", axis=1, tiled=True)[0]
    groups = lax.axis_size("space")
    rows_here = coupling.shape[1]
    offset = lax.axis_index("space") * rows_here
    link_block = arrow_link[0]
    link_rows = lax.dynamic_slice_in_dim(link_block, offset, rows_here, 0)
    succ_rows = next_block[0]
    succ_arrow = next_arrow[0]
    gathered = lax.all_gather(succ_arrow, "space", axis=0, tiled=True)
    carried = jnp.dot(coupling[0], gathered, precision=highest, preferred_element_type=jnp.float32)
    arrow_rows = carried + jnp.dot(
        link_rows, fixed_cov, precision=highest, preferred_element_type=jnp.float32
    )
    cross_turned = jnp.dot(
        succ_rows, panels.T, precision=highest, preferred_element_type=jnp.float32
    )
    cross_turned = cross_turned + jnp.dot(
        succ_arrow, link_block.T, precision=highest, preferred_element_type=jnp.float32
    )
    pieces = (
        cross_turned.reshape(rows_here, groups, rows_here)
        .transpose(2, 1, 0)
        .reshape(rows_here, groups * rows_here)
    )
    cross_rows = lax.all_to_all(pieces, "space", split_axis=1, concat_axis=1, tiled=True)
    diag_rows = local_cov[0] + jnp.dot(
        cross_rows, panels.T, precision=highest, preferred_element_type=jnp.float32
    )
    diag_rows = diag_rows + jnp.dot(
        arrow_rows, link_block.T, precision=highest, preferred_element_type=jnp.float32
    )
    return (diag_rows[None], cross_rows[None], arrow_rows[None])


def solution(mesh):
    return jax.shard_map(
        shards,
        mesh=mesh,
        in_specs=(
            P("tm", "space", None),
            P("tm", None, None),
            P("tm", "space", None),
            P("tm", "space", None),
            P("tm", "space", None),
            P(),
        ),
        out_specs=(P("tm", "space", None), P("tm", "space", None), P("tm", "space", None)),
        check_vma=False,
    )
```

profile of v0, /device:TPU:8, one launch (start us, length us, event | category | flops | bytes accessed | tf_op | source)
XLA Modules:
  0.0 218.1 jit_solution(1109246769169374447)
XLA Ops:
  7.2 0.0 copy-start
  7.2 0.0 copy-start.1
  7.2 0.0 copy-start.4
  7.2 0.0 all-gather.3.cloned.1.call-start
  7.2 0.7 all-gather.3.cloned.1.call-update
  7.9 1.9 collective-permute-start
  9.9 7.8 %collective-permute-start.1 = (f32[1,64,64]{2,1,0:T(8,128)}, f32[1,64,64]{2,1,0:T(8,128)S(1)}, u32[]{:S(2)}, u32[]{:S(2)}) collective-permute-start(f32[1,64,64]{2,1,0:T(8,128)} %param.10), channel_id=1, source_target_pairs={{32,0},{64,32},{96,64},{128,96},{160,128},{192,160},{224,192},{256... | collective-permute-start | bytes 49160 | tf_op jit(solution)/shard_map/ppermute | solution.py:10
  17.7 1.9 collective-permute-done.1
  19.6 0.0 copy-done
  19.6 0.6 fusion.13
  20.2 0.0 collective-permute-done
  20.2 100.1 %all-gather.3.cloned.1.call-done = bf16[1,2048,2048]{2,1,0:T(8,128)(2,1)} async-done(((bf16[1,64,2048]{2,1,0:T(8,128)(2,1)}), bf16[1,2048,2048]{2,1,0:T(8,128)(2,1)}) %all-gather.3.cloned.1.call-update) | async-done | bytes 8388624 | tf_op jit(solution)/shard_map/all_gather | solution.py:16
  120.3 10.0 %fusion.5 = f32[64,2048]{1,0:T(8,128)S(1)} fusion(f32[64,2048]{1,0:T(8,128)S(1)} %fusion.13, bf16[1,2048,2048]{2,1,0:T(8,128)(2,1)} %all-gather.3.cloned.1.call-done, f32[1,64,2048]{2,1,0:T(8,128)S(1)} %collective-permute-done), kind=kOutput, calls=%fused_computation.6 | convolution fusion | flops 3221356544 | bytes 9961472 | tf_op jit(solution)/shard_map/dot_general | solution.py:29
  130.4 0.0 copy-start.2
  130.4 0.3 copy.16
  130.7 1.5 reshape.17
  132.2 5.4 %all-to-all-start = ((f32[32,1,4096]{2,1,0:T(1,128)}), f32[32,1,4096]{2,1,0:T(1,128)S(1)}, u32[]{:S(2)}, u32[]{:S(2)}) async-start(f32[32,1,4096]{2,1,0:T(1,128)} %reshape.17), calls=%async_computation | async-start | bytes 1048576 | tf_op jit(solution)/shard_map/all_to_all | solution.py:40
  137.6 0.0 copy-done.4
  137.6 0.3 fusion.17
  138.0 56.4 %all-gather = f32[1,2048,64]{2,1,0:T(8,128)S(1)} all-gather(f32[1,64,64]{2,1,0:T(8,128)S(1)} %collective-permute-done.1), channel_id=2, replica_groups=mesh['tm'=16,'space'=32] {'space'}, dimensions={1}, use_global_device_ids=true | all-gather | bytes 540672 | tf_op jit(solution)/shard_map/all_gather | solution.py:24
  194.3 0.5 convolution_add_fusion.1
  194.8 0.0 copy-start.3
  194.8 0.0 all-to-all-done
  194.8 0.5 broadcast
  195.3 1.9 reduce
  197.2 0.4 reshape.18
  197.7 0.6 copy.14
  198.3 0.4 all_to_all.7
  198.6 1.2 broadcast_in_dim.10
  199.8 0.0 copy-done.2
  199.8 10.0 %fusion.8 = f32[64,2048]{1,0:T(8,128)S(1)} fusion(f32[64,2048]{1,0:T(8,128)S(1)} %all_to_all.7, bf16[1,2048,2048]{2,1,0:T(8,128)(2,1)} %all-gather.3.cloned.1.call-done, f32[1,64,2048]{2,1,0:T(8,128)S(1)} %copy-done.2), kind=kOutput, calls=%fused_computation.7 | convolution fusion | flops 3221356544 | bytes 9961472 | tf_op jit(solution)/shard_map/dot_general | solution.py:41
  209.9 1.4 fusion.4
  (2 shorter events, 0.0 us)
Async XLA Ops:
  7.2 12.4 %copy-start = (f32[1,2048,64]{1,2,0:T(8,128)S(1)}, f32[1,2048,64]{1,2,0:T(8,128)}, u32[]{:S(2)}) copy-start(f32[1,2048,64]{1,2,0:T(8,128)} %param.7) | copy-start | bytes 1572868
  7.2 187.1 %copy-start.1 = (bf16[1,64,2048]{2,1,0:T(8,128)(2,1)S(1)}, bf16[1,64,2048]{2,1,0:T(8,128)(2,1)}, u32[]{:S(2)}) copy-start(bf16[1,64,2048]{2,1,0:T(8,128)(2,1)} %param.6) | copy-start | bytes 786436
  7.2 130.4 %copy-start.4 = (f32[64,64]{1,0:T(8,128)S(1)}, f32[64,64]{1,0:T(8,128)}, u32[]{:S(2)}) copy-start(f32[64,64]{1,0:T(8,128)} %param.11) | copy-start | bytes 49156
  7.2 113.1 %all-gather.3.cloned.1.call-start = ((), (), s32[]{:S(2)}) async-start(), calls=%async_computation.1 | async-start | bytes 8650752 | tf_op jit(solution)/shard_map/all_gather | solution.py:16
  7.9 12.2 %collective-permute-start = (f32[1,64,2048]{2,1,0:T(8,128)}, f32[1,64,2048]{2,1,0:T(8,128)S(1)}, u32[]{:S(2)}, u32[]{:S(2)}) collective-permute-start(f32[1,64,2048]{2,1,0:T(8,128)} %param.9), channel_id=1, source_target_pairs={{32,0},{64,32},{96,64},{128,96},{160,128},{192,160},{224,192},{256... | collective-permute-start | bytes 1572872 | tf_op jit(solution)/shard_map/ppermute | solution.py:10
  9.9 9.7 %collective-permute-start.1 = (f32[1,64,64]{2,1,0:T(8,128)}, f32[1,64,64]{2,1,0:T(8,128)S(1)}, u32[]{:S(2)}, u32[]{:S(2)}) collective-permute-start(f32[1,64,64]{2,1,0:T(8,128)} %param.10), channel_id=1, source_target_pairs={{32,0},{64,32},{96,64},{128,96},{160,128},{192,160},{224,192},{256... | collective-permute-start | bytes 49160 | tf_op jit(solution)/shard_map/ppermute | solution.py:10
  130.4 69.4 %copy-start.2 = (f32[1,64,2048]{2,1,0:T(8,128)S(1)}, f32[1,64,2048]{2,1,0:T(8,128)}, u32[]{:S(2)}) copy-start(f32[1,64,2048]{2,1,0:T(8,128)} %param.8) | copy-start | bytes 1572868
  132.2 62.7 %all-to-all-start = ((f32[32,1,4096]{2,1,0:T(1,128)}), f32[32,1,4096]{2,1,0:T(1,128)S(1)}, u32[]{:S(2)}, u32[]{:S(2)}) async-start(f32[32,1,4096]{2,1,0:T(1,128)} %reshape.17), calls=%async_computation | async-start | bytes 1048576 | tf_op jit(solution)/shard_map/all_to_all | solution.py:40
  194.8 15.0 %copy-start.3 = (f32[64,64]{1,0:T(8,128)}, f32[64,64]{1,0:T(8,128)S(1)}, u32[]{:S(2)}) copy-start(f32[64,64]{1,0:T(8,128)S(1)} %convolution_add_fusion.1) | copy-start | bytes 49156
Sparse Core Ops, SparseCore 0:
  11.2 109.0 all-gather.2
where the time goes:
time: 218 us
  waiting for transfers between devices  103 us (47%)
  blocking collectives  56.4 us (26%)
  matrix products  22.8 us (10%)
  starting transfers between devices  15.2 us (7%)
  between operations  14.2 us (7%)
  local copies, waits for them, and re-layouts  4.86 us (2%)
    all_gather x1, waiting for transfers between devices, shards(): panels = lax.all_gather(coupling, 'space', axis=1, tiled=True)[0]  100 us
    all_gather x1, blocking collectives, shards(): gathered = lax.all_gather(succ_arrow, 'space', axis=0, tiled=True)  56.4 us
    dot_general x1, matrix products, shards(): jnp.dot(cross_rows, panels.T, precision=highest, preferred_element_type=j...  10 us
    dot_general x1, matrix products, shards(): jnp.dot(succ_rows, panels.T, precision=highest, preferred_element_type=jn...  10 us
    ppermute x2, starting transfers between devices, passed_along(): return lax.ppermute(block, axis, route)  9.75 us
    all_to_all x1, starting transfers between devices, shards(): lax.all_to_all(pieces, 'space', split_axis=1, concat_axis=1, tiled=True)  5.45 us
  transfers between devices with their start and end apart: 4, of which 2 were waited for; matrix products, arithmetic and copies ran while one was open for 1% of the time, Pallas kernels for 0%

commit v1 on v0

--- a/solution.py
+++ b/solution.py
@@ -1,7 +1,18 @@
+import functools
 import jax
 import jax.numpy as jnp
 from jax import lax
 from jax.sharding import PartitionSpec as P
+
+
+def review_the_sums_all(a0, group_axis):
+    heard = lax.axis_size(group_axis)
+    oldest = jnp.stack([a0] * heard)
+    earlier = lax.all_to_all(oldest, axis_name=group_axis, split_axis=0, concat_axis=0)
+    return jnp.concatenate(earlier, 1)
+
+
+mix_thing_for = functools.partial(review_the_sums_all, group_axis="space")
 
 
 def passed_along(block, axis, distance):
@@ -13,7 +24,7 @@
 def shards(coupling, arrow_link, local_cov, boundary_cov, boundary_arrow, fixed_cov):
     highest = lax.Precision.HIGHEST
     next_block, next_arrow = passed_along((boundary_cov, boundary_arrow), "tm", -1)
-    panels = lax.all_gather(coupling, "space", axis=1, tiled=True)[0]
+    panels = mix_thing_for(coupling)[0]
     groups = lax.axis_size("space")
     rows_here = coupling.shape[1]
     offset = lax.axis_index("space") * rows_here

time: 218 us -> 308 us (1.41)
  the two profiles are of different devices: /device:TPU:8 before, /device:TPU:32 now
where the time goes in v1:
time: 308 us; the launch traced here: 307 us
  waiting for transfers between devices  184 us (60%)
  blocking collectives  55.9 us (18%)
  starting transfers between devices  31.9 us (10%)
  matrix products  22.8 us (7%)
  local copies, waits for them, and re-layouts  10.2 us (3%)
    all_to_all x1, waiting for transfers between devices, review_the_sums_all(): lax.all_to_all(oldest, axis_name=group_axis, split_axis=0, concat_axis=0)  179 us
    all_gather x1, blocking collectives, shards(): gathered = lax.all_gather(succ_arrow, 'space', axis=0, tiled=True)  55.9 us
    all_to_all x1, starting transfers between devices, shards(): lax.all_to_all(pieces, 'space', split_axis=1, concat_axis=1, tiled=True)  14 us
    all_to_all x1, starting transfers between devices, review_the_sums_all(): lax.all_to_all(oldest, axis_name=group_axis, split_axis=0, concat_axis=0)  13.4 us
    dot_general x1, matrix products, shards(): jnp.dot(cross_rows, panels.T, precision=highest, preferred_element_type=j...  10 us
    dot_general x1, matrix products, shards(): jnp.dot(succ_rows, panels.T, precision=highest, preferred_element_type=jn...  10 us
  transfers between devices with their start and end apart: 4, of which 2 were waited for; matrix products, arithmetic and copies ran while one was open for 0% of the time, Pallas kernels for 0%

profile of v1, /device:TPU:32, one launch (start us, length us, event | category | flops | bytes accessed | tf_op | source)
XLA Modules:
  0.0 307.2 jit_solution(16801299490468854616)
XLA Ops:
  0.6 0.0 copy-start
  0.6 5.3 %stack.2 = bf16[32,1,64,2048]{3,2,1,0:T(8,128)(2,1)} broadcast(bf16[64,2048]{1,0:T(8,128)(2,1)} %bitcast.38), dimensions={2,3} | broadcast | bytes 8650752 | tf_op jit(solution)/shard_map/stack | solution.py:10
  6.0 13.4 %all-to-all-start = ((bf16[32,1,64,2048]{3,2,1,0:T(8,128)(2,1)}), bf16[32,1,64,2048]{3,2,1,0:T(8,128)(2,1)}, u32[]{:S(2)}, u32[]{:S(2)}) async-start(bf16[32,1,64,2048]{3,2,1,0:T(8,128)(2,1)} %stack.2), calls=%async_computation | async-start | bytes 16777216 | tf_op jit(solution)/shard_map/all_to_all | solution.py:11
  19.4 0.0 copy-done.5
  19.4 0.0 copy-start.4
  19.4 0.0 copy-start.1
  19.4 2.1 collective-permute-start
  21.5 2.5 collective-permute-start.1
  24.0 4.5 %collective-permute-done.1 = f32[1,64,64]{2,1,0:T(8,128)S(1)} collective-permute-done((f32[1,64,64]{2,1,0:T(8,128)S(1)}, f32[1,64,64]{2,1,0:T(8,128)S(1)}, u32[]{:S(2)}, u32[]{:S(2)}) %collective-permute-start.1) | collective-permute-done | bytes 16416 | tf_op jit(solution)/shard_map/ppermute | solution.py:21
  28.5 0.6 fusion.3
  29.1 0.0 collective-permute-done
  29.1 179.1 %all-to-all-done = bf16[32,1,64,2048]{3,2,1,0:T(8,128)(2,1)} async-done(((bf16[32,1,64,2048]{3,2,1,0:T(8,128)(2,1)}), bf16[32,1,64,2048]{3,2,1,0:T(8,128)(2,1)}, u32[]{:S(2)}, u32[]{:S(2)}) %all-to-all-start) | async-done | bytes 8388640 | tf_op jit(solution)/shard_map/all_to_all | solution.py:11
  208.2 10.0 %convolution_add_fusion.2 = f32[64,2048]{1,0:T(8,128)S(1)} fusion(f32[64,2048]{1,0:T(8,128)S(1)} %fusion.3, bf16[2048,2048]{1,0:T(8,128)(2,1)} %bitcast.3, f32[1,64,2048]{2,1,0:T(8,128)S(1)} %collective-permute-done), kind=kOutput, calls=%fused_computation.2 | convolution fusion | flops 3221356544 | bytes 9961472 | tf_op jit(solution)/shard_map/dot_general | solution.py:40
  218.2 0.0 copy-start.2
  218.2 0.3 copy.16
  218.6 1.5 reshape.20
  220.0 14.0 %all-to-all-start.1 = ((f32[32,1,4096]{2,1,0:T(1,128)}), f32[32,1,4096]{2,1,0:T(1,128)S(1)}, u32[]{:S(2)}, u32[]{:S(2)}) async-start(f32[32,1,4096]{2,1,0:T(1,128)} %reshape.20), calls=%async_computation.1 | async-start | bytes 1048576 | tf_op jit(solution)/shard_map/all_to_all | solution.py:51
  234.0 0.0 copy-done.4
  234.0 0.3 fusion.6
  234.3 55.9 %all-gather = f32[1,2048,64]{2,1,0:T(8,128)S(1)} all-gather(f32[1,64,64]{2,1,0:T(8,128)S(1)} %collective-permute-done.1), channel_id=2, replica_groups=mesh['tm'=16,'space'=32] {'space'}, dimensions={1}, use_global_device_ids=true | all-gather | bytes 540672 | tf_op jit(solution)/shard_map/all_gather | solution.py:35
  290.3 0.5 convolution_add_fusion.3
  290.8 0.0 copy-start.3
  290.8 0.0 all-to-all-done.1
  290.8 0.5 broadcast.3
  291.3 1.9 reduce
  293.2 0.4 reshape.21
  293.6 0.6 copy.14
  294.3 0.4 all_to_all.11
  294.6 1.2 broadcast_in_dim.10
  295.8 0.0 copy-done.2
  295.8 10.0 %convolution_add_fusion.1 = f32[64,2048]{1,0:T(8,128)S(1)} fusion(f32[64,2048]{1,0:T(8,128)S(1)} %all_to_all.11, bf16[2048,2048]{1,0:T(8,128)(2,1)} %bitcast.3, f32[1,64,2048]{2,1,0:T(8,128)S(1)} %copy-done.2), kind=kOutput, calls=%fused_computation.1 | convolution fusion | flops 3221356544 | bytes 9961472 | tf_op jit(solution)/shard_map/dot_general | solution.py:52
  305.8 1.4 fusion
  (6 shorter events, 0.0 us)
Async XLA Ops:
  0.6 27.9 %copy-start = (f32[1,2048,64]{1,2,0:T(8,128)S(1)}, f32[1,2048,64]{1,2,0:T(8,128)}, u32[]{:S(2)}) copy-start(f32[1,2048,64]{1,2,0:T(8,128)} %param.7) | copy-start | bytes 1572868
  6.0 13.4 %copy-start.5 = (f32[1,64,2048]{2,1,0:T(8,128)S(1)}, f32[1,64,2048]{2,1,0:T(8,128)}, u32[]{:S(2)}) copy-start(f32[1,64,2048]{2,1,0:T(8,128)} %param.9) | copy-start | bytes 1572868
  6.0 15.5 %copy-start.6 = (f32[1,64,64]{2,1,0:T(8,128)S(1)}, f32[1,64,64]{2,1,0:T(8,128)}, u32[]{:S(2)}) copy-start(f32[1,64,64]{2,1,0:T(8,128)} %param.10) | copy-start | bytes 49156
  6.0 202.2 %all-to-all-start = ((bf16[32,1,64,2048]{3,2,1,0:T(8,128)(2,1)}), bf16[32,1,64,2048]{3,2,1,0:T(8,128)(2,1)}, u32[]{:S(2)}, u32[]{:S(2)}) async-start(bf16[32,1,64,2048]{3,2,1,0:T(8,128)(2,1)} %stack.2), calls=%async_computation | async-start | bytes 16777216 | tf_op jit(solution)/shard_map/all_to_all | solution.py:11
  19.4 214.6 %copy-start.4 = (f32[64,64]{1,0:T(8,128)S(1)}, f32[64,64]{1,0:T(8,128)}, u32[]{:S(2)}) copy-start(f32[64,64]{1,0:T(8,128)} %param.11) | copy-start | bytes 49156
  19.4 270.9 %copy-start.1 = (bf16[1,64,2048]{2,1,0:T(8,128)(2,1)S(1)}, bf16[1,64,2048]{2,1,0:T(8,128)(2,1)}, u32[]{:S(2)}) copy-start(bf16[1,64,2048]{2,1,0:T(8,128)(2,1)} %param.6) | copy-start | bytes 786436
  19.4 9.7 %collective-permute-start = (f32[1,64,2048]{2,1,0:T(8,128)S(1)}, f32[1,64,2048]{2,1,0:T(8,128)S(1)}, u32[]{:S(2)}, u32[]{:S(2)}) collective-permute-start(f32[1,64,2048]{2,1,0:T(8,128)S(1)} %copy-done.5), channel_id=1, source_target_pairs={{32,0},{64,32},{96,64},{128,96},{160,128},{192,160},{224,192},{256... | collective-permute-start | bytes 1572872 | tf_op jit(solution)/shard_map/ppermute | solution.py:21
  21.5 7.0 %collective-permute-start.1 = (f32[1,64,64]{2,1,0:T(8,128)S(1)}, f32[1,64,64]{2,1,0:T(8,128)S(1)}, u32[]{:S(2)}, u32[]{:S(2)}) collective-permute-start(f32[1,64,64]{2,1,0:T(8,128)S(1)} %copy-done.6), channel_id=1, source_target_pairs={{32,0},{64,32},{96,64},{128,96},{160,128},{192,160},{224,192},{256... | collective-permute-start | bytes 49160 | tf_op jit(solution)/shard_map/ppermute | solution.py:21
  218.2 77.5 %copy-start.2 = (f32[1,64,2048]{2,1,0:T(8,128)S(1)}, f32[1,64,2048]{2,1,0:T(8,128)}, u32[]{:S(2)}) copy-start(f32[1,64,2048]{2,1,0:T(8,128)} %param.8) | copy-start | bytes 1572868
  220.0 70.8 %all-to-all-start.1 = ((f32[32,1,4096]{2,1,0:T(1,128)}), f32[32,1,4096]{2,1,0:T(1,128)S(1)}, u32[]{:S(2)}, u32[]{:S(2)}) async-start(f32[32,1,4096]{2,1,0:T(1,128)} %reshape.20), calls=%async_computation.1 | async-start | bytes 1048576 | tf_op jit(solution)/shard_map/all_to_all | solution.py:51
  290.8 15.0 %copy-start.3 = (f32[64,64]{1,0:T(8,128)}, f32[64,64]{1,0:T(8,128)S(1)}, u32[]{:S(2)}) copy-start(f32[64,64]{1,0:T(8,128)S(1)} %convolution_add_fusion.3) | copy-start | bytes 49156

commit v2 on v0

--- a/solution.py
+++ b/solution.py
@@ -37,7 +37,10 @@
         .transpose(2, 1, 0)
         .reshape(rows_here, groups * rows_here)
     )
-    cross_rows = lax.all_to_all(pieces, "space", split_axis=1, concat_axis=1, tiled=True)
+    size = lax.axis_size("space")
+    blocks = jnp.stack(jnp.split(pieces, size, axis=1), axis=0)
+    blocks = lax.all_to_all(blocks, "space", split_axis=0, concat_axis=0)
+    cross_rows = jnp.concatenate(blocks, axis=1)
     diag_rows = local_cov[0] + jnp.dot(
         cross_rows, panels.T, precision=highest, preferred_element_type=jnp.float32
     )

time: 218 us -> 221 us (1.014)
  local copies, waits for them, and re-layouts: 4.86 us -> 7.68 us
where the time goes in v2:
time: 221 us
  waiting for transfers between devices  103 us (47%)
  blocking collectives  56.4 us (26%)
  matrix products  22.8 us (10%)
  starting transfers between devices  15.2 us (7%)
  between operations  14.3 us (6%)
  local copies, waits for them, and re-layouts  7.68 us (3%)
    all_gather x1, waiting for transfers between devices, shards(): panels = lax.all_gather(coupling, 'space', axis=1, tiled=True)[0]  100 us
    all_gather x1, blocking collectives, shards(): gathered = lax.all_gather(succ_arrow, 'space', axis=0, tiled=True)  56.4 us
    dot_general x1, matrix products, shards(): jnp.dot(cross_rows, panels.T, precision=highest, preferred_element_type=j...  10 us
    dot_general x1, matrix products, shards(): jnp.dot(succ_rows, panels.T, precision=highest, preferred_element_type=jn...  10 us
    ppermute x2, starting transfers between devices, passed_along(): return lax.ppermute(block, axis, route)  9.75 us
    all_to_all x1, starting transfers between devices, shards(): blocks = lax.all_to_all(blocks, 'space', split_axis=0, concat_axis=0)  5.44 us
  transfers between devices with their start and end apart: 4, of which 2 were waited for; matrix products, arithmetic and copies ran while one was open for 1% of the time, Pallas kernels for 0%

profile of v2, /device:TPU:8, one launch (start us, length us, event | category | flops | bytes accessed | tf_op | source)
XLA Modules:
  0.0 221.0 jit_solution(16883251507901689929)
XLA Ops:
  7.2 0.7 all-gather.3.cloned.1.call-update
  7.9 1.9 collective-permute-start
  9.8 7.8 %collective-permute-start.1 = (f32[1,64,64]{2,1,0:T(8,128)}, f32[1,64,64]{2,1,0:T(8,128)S(1)}, u32[]{:S(2)}, u32[]{:S(2)}) collective-permute-start(f32[1,64,64]{2,1,0:T(8,128)} %param.10), channel_id=1, source_target_pairs={{32,0},{64,32},{96,64},{128,96},{160,128},{192,160},{224,192},{256... | collective-permute-start | bytes 49160 | tf_op jit(solution)/shard_map/ppermute | solution.py:10
  17.7 1.9 collective-permute-done.1
  19.6 0.6 fusion.13
  20.2 100.1 %all-gather.3.cloned.1.call-done = bf16[1,2048,2048]{2,1,0:T(8,128)(2,1)} async-done(((bf16[1,64,2048]{2,1,0:T(8,128)(2,1)}), bf16[1,2048,2048]{2,1,0:T(8,128)(2,1)}) %all-gather.3.cloned.1.call-update) | async-done | bytes 8388624 | tf_op jit(solution)/shard_map/all_gather | solution.py:16
  120.3 10.0 %fusion.5 = f32[64,2048]{1,0:T(8,128)S(1)} fusion(f32[64,2048]{1,0:T(8,128)S(1)} %fusion.13, bf16[1,2048,2048]{2,1,0:T(8,128)(2,1)} %all-gather.3.cloned.1.call-done, f32[1,64,2048]{2,1,0:T(8,128)S(1)} %collective-permute-done), kind=kOutput, calls=%fused_computation.6 | convolution fusion | flops 3221356544 | bytes 9961472 | tf_op jit(solution)/shard_map/dot_general | solution.py:29
  130.3 0.4 reshape.19
  130.8 1.1 copy.41
  131.9 0.4 reshape.20
  132.2 0.1 constant_dynamic-update-slice_fusion.30
  132.3 0.1 constant_dynamic-update-slice_fusion.28
  132.4 0.1 constant_dynamic-update-slice_fusion.26
  132.7 0.1 constant_dynamic-update-slice_fusion.20
  132.8 0.1 constant_dynamic-update-slice_fusion.18
  132.8 0.1 constant_dynamic-update-slice_fusion.16
  133.2 0.1 constant_dynamic-update-slice_fusion.8
  133.3 0.1 constant_dynamic-update-slice_fusion.6
  133.3 0.1 constant_dynamic-update-slice_fusion.4
  133.6 1.4 reshape.24
  135.0 5.4 %all-to-all-start = ((f32[32,1,4096]{2,1,0:T(1,128)}), f32[32,1,4096]{2,1,0:T(1,128)S(1)}, u32[]{:S(2)}, u32[]{:S(2)}) async-start(f32[32,1,4096]{2,1,0:T(1,128)} %reshape.24), calls=%async_computation | async-start | bytes 1048576 | tf_op jit(solution)/shard_map/all_to_all | solution.py:42
  140.5 0.3 fusion.17
  140.8 56.4 %all-gather = f32[1,2048,64]{2,1,0:T(8,128)S(1)} all-gather(f32[1,64,64]{2,1,0:T(8,128)S(1)} %collective-permute-done.1), channel_id=2, replica_groups=mesh['tm'=16,'space'=32] {'space'}, dimensions={1}, use_global_device_ids=true | all-gather | bytes 540672 | tf_op jit(solution)/shard_map/all_gather | solution.py:24
  197.2 0.5 convolution_add_fusion.1
  197.7 0.5 broadcast
  198.2 1.9 reduce
  200.1 0.4 reshape.25
  200.5 0.6 copy.42
  201.2 0.4 reshape.22
  201.5 1.2 broadcast_in_dim_reshape.3
  202.7 10.0 %fusion.8 = f32[64,2048]{1,0:T(8,128)S(1)} fusion(f32[64,2048]{1,0:T(8,128)S(1)} %reshape.22, bf16[1,2048,2048]{2,1,0:T(8,128)(2,1)} %all-gather.3.cloned.1.call-done, f32[1,64,2048]{2,1,0:T(8,128)S(1)} %copy-done.2), kind=kOutput, calls=%fused_computation.7 | convolution fusion | flops 3221356544 | bytes 9961472 | tf_op jit(solution)/shard_map/dot_general | solution.py:44
  212.7 1.4 fusion.4
  (36 shorter events, 0.7 us)
Async XLA Ops:
  7.2 12.4 %copy-start = (f32[1,2048,64]{1,2,0:T(8,128)S(1)}, f32[1,2048,64]{1,2,0:T(8,128)}, u32[]{:S(2)}) copy-start(f32[1,2048,64]{1,2,0:T(8,128)} %param.7) | copy-start | bytes 1572868
  7.2 113.1 %all-gather.3.cloned.1.call-start = ((), (), s32[]{:S(2)}) async-start(), calls=%async_computation.1 | async-start | bytes 8650752 | tf_op jit(solution)/shard_map/all_gather | solution.py:16
  7.9 12.3 %collective-permute-start = (f32[1,64,2048]{2,1,0:T(8,128)}, f32[1,64,2048]{2,1,0:T(8,128)S(1)}, u32[]{:S(2)}, u32[]{:S(2)}) collective-permute-start(f32[1,64,2048]{2,1,0:T(8,128)} %param.9), channel_id=1, source_target_pairs={{32,0},{64,32},{96,64},{128,96},{160,128},{192,160},{224,192},{256... | collective-permute-start | bytes 1572872 | tf_op jit(solution)/shard_map/ppermute | solution.py:10
  9.8 9.7 %collective-permute-start.1 = (f32[1,64,64]{2,1,0:T(8,128)}, f32[1,64,64]{2,1,0:T(8,128)S(1)}, u32[]{:S(2)}, u32[]{:S(2)}) collective-permute-start(f32[1,64,64]{2,1,0:T(8,128)} %param.10), channel_id=1, source_target_pairs={{32,0},{64,32},{96,64},{128,96},{160,128},{192,160},{224,192},{256... | collective-permute-start | bytes 49160 | tf_op jit(solution)/shard_map/ppermute | solution.py:10
  20.2 120.3 %copy-start.4 = (f32[64,64]{1,0:T(8,128)S(1)}, f32[64,64]{1,0:T(8,128)}, u32[]{:S(2)}) copy-start(f32[64,64]{1,0:T(8,128)} %param.11) | copy-start | bytes 49156
  20.2 177.0 %copy-start.1 = (bf16[1,64,2048]{2,1,0:T(8,128)(2,1)S(1)}, bf16[1,64,2048]{2,1,0:T(8,128)(2,1)}, u32[]{:S(2)}) copy-start(bf16[1,64,2048]{2,1,0:T(8,128)(2,1)} %param.6) | copy-start | bytes 786436
  131.9 70.8 %copy-start.2 = (f32[1,64,2048]{2,1,0:T(8,128)S(1)}, f32[1,64,2048]{2,1,0:T(8,128)}, u32[]{:S(2)}) copy-start(f32[1,64,2048]{2,1,0:T(8,128)} %param.8) | copy-start | bytes 1572868
  135.0 62.6 %all-to-all-start = ((f32[32,1,4096]{2,1,0:T(1,128)}), f32[32,1,4096]{2,1,0:T(1,128)S(1)}, u32[]{:S(2)}, u32[]{:S(2)}) async-start(f32[32,1,4096]{2,1,0:T(1,128)} %reshape.24), calls=%async_computation | async-start | bytes 1048576 | tf_op jit(solution)/shard_map/all_to_all | solution.py:42
  197.7 15.0 %copy-start.3 = (f32[64,64]{1,0:T(8,128)}, f32[64,64]{1,0:T(8,128)S(1)}, u32[]{:S(2)}) copy-start(f32[64,64]{1,0:T(8,128)S(1)} %convolution_add_fusion.1) | copy-start | bytes 49156
Sparse Core Ops, SparseCore 0:
  11.2 109.0 all-gather.2
